TPU v7x, 32 devices: a whole 2x2x4 slice. The times are simulated.
32 devices in a mesh: ctx: 32 (over z, y, x, core), vocab: 1.
Axes of the slice: x: 2, y: 2, z: 4, core: 2. Of those that a mesh axis runs over, the one named last changes fastest.
Arguments:
- hidden_states: bfloat16 [8192, 8192], P('ctx'), may hold values from -24 to 24
- master: float32 [128, 8192], P(('vocab', 'ctx')), may hold values from -1 to 1
- moment: float32 [128, 8192], P(('vocab', 'ctx')), may hold values from -6 to 6
- second: float32 [128, 8192], P(('vocab', 'ctx')), may hold values from 0.05 to 5
- targets: int32 [8192], P('ctx'), may hold values from 0 to 255, as said below
- loss_mask: int32 [8192], P('ctx'), may hold values from 0 to 1, as said below
- prior_lse: float32 [8192], P('ctx'), may hold values from 6 to 9
- prior_target: float32 [8192], P('ctx'), may hold values from -5 to 5
- span_order: int32 [64], replicated, may hold values from 0 to 63, as said below
Outputs:
- token_loss: float32 [8192], P('ctx')
- mean_loss: float32 [], replicated
- hidden_grad: bfloat16 [8192, 8192], P('ctx', 'vocab')
- new_master: float32 [128, 8192], P(('vocab', 'ctx'))
- new_moment: float32 [128, 8192], P(('vocab', 'ctx'))
- new_second: float32 [128, 8192], P(('vocab', 'ctx'))
Inputs may be any that keep to these rules, and one draw needn't show every extreme that they name: `targets`: ids of 128 and more fall in this block, id minus 128 naming its row; smaller ids lie in earlier blocks. `loss_mask`: 1 on a leading run of the slab's positions and 0 after it; at least 2048 ones. `span_order`: each span number once.
All inputs are finite; a program needn't handle non-finite values.
Results may differ from a plain program's by a relative error of at most 0.0085.
Values may be sent and summed in bfloat16 or wider, within the bound.
A program may use at most 128 MiB of HBM per device.

v0:
```python
import jax
import jax.numpy as jnp
from jax import lax
from jax.sharding import PartitionSpec as P

loss_scale = 1048576.0
clip_norm = 0.004
beta_one = 0.9
beta_two = 0.95
learn_rate = 0.001
weight_decay = 0.1
adam_eps = 1e-08


def project(block_rows, weight_rows):
    return lax.dot_general(
        block_rows, weight_rows, (((1,), (1,)), ((), ())), preferred_element_type=jnp.float32
    )


def body(
    hidden_states, master, moment, second, targets, loss_mask, prior_lse, prior_target, span_order
):
    tok_rows, feat_dim = hidden_states.shape
    shard_rows = master.shape[0]
    ctx_count = lax.axis_size("ctx")
    vocab_count = lax.axis_size("vocab")
    ctx_place = lax.axis_index("ctx")
    vocab_place = lax.axis_index("vocab")
    half_rows = tok_rows // 2
    group_rows = shard_rows * ctx_count
    block_total = group_rows * vocab_count
    head_rows = master.astype(jnp.bfloat16)
    all_targets, all_mask, all_prior, all_outside = (
        lax.all_gather(targets, "ctx", axis=0, tiled=True),
        lax.all_gather(loss_mask, "ctx", axis=0, tiled=True),
        lax.all_gather(prior_lse, "ctx", axis=0, tiled=True),
        lax.all_gather(prior_target, "ctx", axis=0, tiled=True),
    )

    def own_rows(whole):
        pieces = [
            lax.dynamic_slice_in_dim(
                whole, span_order[2 * ctx_place + offset] * half_rows, half_rows, 0
            )
            for offset in (0, 1)
        ]
        return jnp.concatenate(pieces, 0)

    tgt_rows = own_rows(all_targets)
    mask_rows = own_rows(all_mask).astype(jnp.float32)
    prior_rows = own_rows(all_prior)
    outside = own_rows(all_outside)
    local_col = tgt_rows - block_total - vocab_place * group_rows
    token_count = jnp.sum(all_mask.astype(jnp.float32))

    def hit_table(col_count):
        columns = jnp.arange(col_count, dtype=jnp.int32)
        return columns[None, :] == local_col[:, None]

    initial = (
        prior_rows,
        jnp.zeros((tok_rows,), jnp.float32),
        jnp.zeros((tok_rows,), jnp.float32),
        jnp.zeros((tok_rows, group_rows), jnp.float32),
    )
    weight_rows = lax.all_gather(head_rows, "ctx", axis=0, tiled=True)
    block_logits = project(hidden_states, weight_rows)
    new_top = jnp.maximum(initial[0], jnp.max(block_logits, axis=1))
    new_sum = initial[1] * jnp.exp(initial[0] - new_top) + jnp.sum(
        jnp.exp(block_logits - new_top[:, None]), axis=1
    )
    new_target = jnp.sum(jnp.where(hit_table(weight_rows.shape[0]), block_logits, 0.0), axis=1)
    top_value = lax.pmax(new_top, "vocab")
    sum_total, target_sum = lax.psum((new_sum * jnp.exp(new_top - top_value), new_target), "vocab")
    log_total = top_value + jnp.log(jnp.exp(prior_rows - top_value) + sum_total)
    target_logit = jnp.where(tgt_rows >= block_total, target_sum, outside)
    loss_rows = mask_rows * (log_total - target_logit)
    grad_scale = loss_scale / token_count
    onehot = hit_table(group_rows).astype(jnp.float32)
    dlogits = (
        mask_rows[:, None] * (jnp.exp(block_logits - log_total[:, None]) - onehot) * grad_scale
    ).astype(jnp.bfloat16)
    columns = dlogits
    row_grad = lax.psum_scatter(
        lax.dot_general(
            columns, hidden_states, (((0,), (0,)), ((), ())), preferred_element_type=jnp.float32
        ),
        "ctx",
        scatter_dimension=0,
        tiled=True,
    )
    columns = dlogits
    partial_value = jnp.dot(
        columns,
        lax.all_gather(head_rows, "ctx", axis=0, tiled=True),
        preferred_element_type=jnp.float32,
    )
    hidden_grad = lax.psum_scatter(
        partial_value.astype(jnp.bfloat16), "vocab", scatter_dimension=1, tiled=True
    )
    all_losses = lax.all_gather(loss_rows, "ctx", axis=0, tiled=True)
    mean_loss = jnp.sum(all_losses) / token_count
    slot_ids = jnp.arange(span_order.shape[0], dtype=jnp.int32)
    natural = []
    for offset in (0, 1):
        span_id = 2 * ctx_place + offset
        slot_place = jnp.sum(jnp.where(span_order == span_id, slot_ids, 0))
        natural.append(lax.dynamic_slice_in_dim(all_losses, slot_place * half_rows, half_rows, 0))
    token_loss = jnp.concatenate(natural, 0)
    square_sum = lax.psum(jnp.sum(row_grad * row_grad), ("ctx", "vocab"))
    norm_value = jnp.sqrt(square_sum) / loss_scale
    clip_factor = jnp.minimum(1.0, clip_norm / (norm_value + 1e-06))
    clipped = row_grad * clip_factor
    new_moment = beta_one * moment + (1.0 - beta_one) * clipped
    new_second = beta_two * second + (1.0 - beta_two) * clipped * clipped
    new_master = master - learn_rate * (
        new_moment / (jnp.sqrt(new_second) + adam_eps) + weight_decay * master
    )
    return (token_loss, mean_loss, hidden_grad, new_master, new_moment, new_second)


def solution(mesh):
    in_specs = (
        P("ctx", None),
        P(("vocab", "ctx"), None),
        P(("vocab", "ctx"), None),
        P(("vocab", "ctx"), None),
        P("ctx"),
        P("ctx"),
        P("ctx"),
        P("ctx"),
        P(),
    )
    out_specs = (
        P("ctx"),
        P(),
        P("ctx", "vocab"),
        P(("vocab", "ctx"), None),
        P(("vocab", "ctx"), None),
        P(("vocab", "ctx"), None),
    )
    return jax.shard_map(body, mesh=mesh, in_specs=in_specs, out_specs=out_specs, check_vma=False)
```

profile of v0, /device:TPU:0, one launch (start us, length us, event | category | flops | bytes accessed | tf_op | source)
XLA Modules:
  0.0 370.4 jit_solution(5717343904908202266)
XLA Ops:
  7.2 0.0 all-gather.8.cloned.1.call-start
  7.2 1.6 convert_bitcast_fusion
  8.8 0.0 all-gather.8.cloned.1.call-update
  8.8 0.0 all-reduce.3.cloned.1.call-start
  8.8 1.3 fusion.13
  11.5 43.5 %all-gather = s32[32,1,256]{2,1,0:T(1,128)S(1)} all-gather(s32[1,1,256]{2,1,0:T(1,128)} %bitcast.25), channel_id=1, replica_groups=mesh['ctx'=32,'vocab'=1] {'ctx'}, dimensions={0}, use_global_device_ids=true | all-gather | bytes 33792 | tf_op jit(solution)/shard_map/all_gather | solution.py:36
  55.0 0.6 convert_reduce_fusion
  56.3 36.9 %all-gather.1 = f32[32,1,256]{2,1,0:T(1,128)S(1)} all-gather(f32[1,1,256]{2,1,0:T(1,128)} %bitcast.26), channel_id=1, replica_groups=mesh['ctx'=32,'vocab'=1] {'ctx'}, dimensions={0}, use_global_device_ids=true | all-gather | bytes 33792 | tf_op jit(solution)/shard_map/all_gather | solution.py:37
  93.2 38.2 %all-gather.3 = s32[32,1,256]{2,1,0:T(1,128)S(1)} all-gather(s32[1,1,256]{2,1,0:T(1,128)} %bitcast.27), channel_id=1, replica_groups=mesh['ctx'=32,'vocab'=1] {'ctx'}, dimensions={0}, use_global_device_ids=true | all-gather | bytes 33792 | tf_op jit(solution)/shard_map/all_gather | solution.py:35
  131.5 36.9 %all-gather.4 = f32[32,1,256]{2,1,0:T(1,128)S(1)} all-gather(f32[1,1,256]{2,1,0:T(1,128)} %bitcast.28), channel_id=1, replica_groups=mesh['ctx'=32,'vocab'=1] {'ctx'}, dimensions={0}, use_global_device_ids=true | all-gather | bytes 33792 | tf_op jit(solution)/shard_map/all_gather | solution.py:38
  168.3 0.1 fusion.9
  168.4 0.1 fusion.11
  168.5 0.1 fusion.12
  168.6 0.1 fusion.10
  168.7 0.0 all-gather.8.cloned.1.call-done
  168.7 2.5 reshape.102
  171.2 0.0 copy-start
  171.3 3.9 %fusion.14 = (f32[256]{0:T(256)S(1)}, f32[256,128]{0,1:T(8,128)S(1)}) fusion(bf16[256,8192]{1,0:T(8,128)(2,1)} %param.9, bf16[128,8192]{1,0:T(8,128)(2,1)S(1)} %reshape.102), kind=kOutput, calls=%fused_computation.33 | convolution fusion | flops 536903424 | bytes 6423552 | tf_op jit(solution)/shard_map/dot_general | solution.py:16
  175.2 0.1 select_reduce_fusion
  175.3 2.7 fusion.6
  178.0 0.0 all-reduce.3.cloned.1.call-update
  178.1 0.6 copy-done.4
  178.7 0.6 fusion.3
  180.6 38.1 %all-gather.5 = f32[32,1,256]{2,1,0:T(1,128)S(1)} all-gather(f32[1,1,256]{2,1,0:T(1,128)S(1)} %bitcast.24), channel_id=1, replica_groups=mesh['ctx'=32,'vocab'=1] {'ctx'}, dimensions={0}, use_global_device_ids=true | all-gather | bytes 33792 | tf_op jit(solution)/shard_map/all_gather | solution.py:102
  218.7 0.7 reduce_sum.67
  219.4 0.1 fusion.8
  219.4 0.6 pad_maximum_fusion.1
  220.0 3.3 convolution_convert_fusion
  223.3 94.3 %all-reduce.3.cloned.1.call-done = f32[128,8192]{1,0:T(8,128)} async-done(((f32[128,8192]{1,0:T(8,128)}), f32[128,8192]{1,0:T(8,128)}) %all-reduce.3.cloned.1.call-update) | async-done | bytes 4194320
  317.6 1.6 multiply_reduce_fusion
  320.5 39.3 %psum.6 = f32[]{:T(128)} all-reduce(f32[]{:T(128)} %multiply_reduce_fusion), channel_id=1, replica_groups=mesh['ctx'=32,'vocab'=1] {'ctx','vocab'}, use_global_device_ids=true, to_apply=%region_9.10 | all-reduce | flops 1 | bytes 8 | tf_op jit(solution)/shard_map/psum | solution.py:111
  360.6 1.9 multiply_subtract_fusion
  (12 shorter events, 0.1 us)
Async XLA Ops:
  7.2 161.5 %all-gather.8.cloned.1.call-start = ((), (), s32[]{:S(2)}) async-start(), calls=%async_computation | async-start | bytes 2162688 | tf_op jit(solution)/shard_map/all_gather | solution.py:67
  8.8 308.8 %all-reduce.3.cloned.1.call-start = ((), (), s32[]{:S(2)}) async-start(), calls=%async_computation.1 | async-start | bytes 8388608
  171.2 4.1 %copy-start = (bf16[256,8192]{1,0:T(8,128)(2,1)S(1)}, bf16[256,8192]{1,0:T(8,128)(2,1)}, u32[]{:S(2)}) copy-start(bf16[256,8192]{1,0:T(8,128)(2,1)} %param.9) | copy-start | bytes 12582916
  178.0 0.7 copy-start.4
  178.0 182.5 %copy-start.1 = (f32[4,8192]{1,0:T(4,128)S(1)}, f32[4,8192]{1,0:T(4,128)}, u32[]{:S(2)}) copy-start(f32[4,8192]{1,0:T(4,128)} %param.10) | copy-start | bytes 393220
  178.1 182.5 %copy-start.2 = (f32[4,8192]{1,0:T(4,128)S(1)}, f32[4,8192]{1,0:T(4,128)}, u32[]{:S(2)}) copy-start(f32[4,8192]{1,0:T(4,128)} %param.12) | copy-start | bytes 393220
  178.1 182.5 %copy-start.3 = (f32[4,8192]{1,0:T(4,128)S(1)}, f32[4,8192]{1,0:T(4,128)}, u32[]{:S(2)}) copy-start(f32[4,8192]{1,0:T(4,128)} %param.11) | copy-start | bytes 393220
Sparse Core Ops, SparseCore 0:
  11.4 59.1 all-gather.7
  178.2 139.3 all-reduce.2
where the time goes:
time: 371 us; the launch traced here: 370 us
  blocking collectives  233 us (63%)
  waiting for transfers between devices  94.3 us (25%)
  between operations  20.7 us (6%)
  matrix products  9.96 us (3%)
  other arithmetic  7.64 us (2%)
  local copies, waits for them, and re-layouts  4.86 us (1%)
    unnamed x3, waiting for transfers between devices  94.3 us
    all_gather x1, blocking collectives, body(): lax.all_gather(loss_mask, 'ctx', axis=0, tiled=True)  43.5 us
    psum x1, blocking collectives, body(): square_sum = lax.psum(jnp.sum(row_grad * row_grad), ('ctx', 'vocab'))  39.3 us
    all_gather x1, blocking collectives, body(): lax.all_gather(targets, 'ctx', axis=0, tiled=True)  38.2 us
    all_gather x1, blocking collectives, body(): all_losses = lax.all_gather(loss_rows, 'ctx', axis=0, tiled=True)  38.1 us
    all_gather x1, blocking collectives, body(): lax.all_gather(prior_lse, 'ctx', axis=0, tiled=True)  36.9 us
    all_gather x1, blocking collectives, body(): lax.all_gather(prior_target, 'ctx', axis=0, tiled=True)  36.9 us
  transfers between devices with their start and end apart: 2, of which 1 were waited for; matrix products, arithmetic and copies ran while one was open for 2% of the time, Pallas kernels for 0%

commit v1 on v0

--- a/solution.py
+++ b/solution.py
@@ -1,6 +1,10 @@
+import functools
+
 import jax
 import jax.numpy as jnp
 from jax import lax
+from jax.experimental import pallas as pl
+from jax.experimental.pallas import tpu as pltpu
 from jax.sharding import PartitionSpec as P
 
 loss_scale = 1048576.0
@@ -18,7 +22,7 @@
     )
 
 
-def body(
+def plain_body(
     hidden_states, master, moment, second, targets, loss_mask, prior_lse, prior_target, span_order
 ):
     tok_rows, feat_dim = hidden_states.shape
@@ -120,6 +124,409 @@
     return (token_loss, mean_loss, hidden_grad, new_master, new_moment, new_second)
 
 
+MESH = pl.DeviceIdType.MESH
+PLANE = 8
+SITES = 4
+FOLD = 16
+CHUNKS = 4
+
+
+def fits(shape):
+    count = shape["ctx"]
+    return shape["vocab"] == 1 and count >= 2 * PLANE and count & (count - 1) == 0
+
+
+def log2(value):
+    return value.bit_length() - 1
+
+
+def kernel(
+    n, shard_rows, order_ref, stats_ref, mst_ref, mom_ref, sec_ref, hid_hbm,
+    tl_ref, ml_ref, hg_hbm, nmst_ref, nmom_ref, nsec_ref,
+    hid, hg, fold32, wg, w, lg, dl, dlt, st, lb, sqb, sb0, rb0, acc, sb1, rb1, sb2, rb2, gb,
+    hin_sem, hout_sem, zs, zr, ps, pr, bs, br, sts, str_, lbs, lbr, sqs, sqr,
+    r0s, r0r, r1s, r1r, r2s, r2r,
+):
+    f32, bf16 = jnp.float32, jnp.bfloat16
+    nz = n // PLANE
+    feat = hid.shape[1]
+    tok = hid.shape[0]
+    half_tok = tok // 2
+    pieces = FOLD // shard_rows
+    cols = feat // pieces
+    cc = feat // CHUNKS
+    half_rows = shard_rows * SITES * nz
+    group_rows = 2 * half_rows
+    me = lax.axis_index("ctx")
+    core = lax.rem(me, 2)
+    site = lax.rem(lax.div(me, 2), SITES)
+    z = lax.div(me, PLANE)
+    sib = me + 1 - 2 * core
+
+    def slot(c, s, k):
+        return (c * SITES + s) * nz + k
+
+    def back(v, d, m):
+        return lax.rem(v - d + m, m)
+
+    def fwd(v, d, m):
+        return lax.rem(v + d, m)
+
+    def rcopy(src, dst, ssem, rsem, dev):
+        return pltpu.make_async_remote_copy(
+            src_ref=src, dst_ref=dst, send_sem=ssem, recv_sem=rsem,
+            device_id={"ctx": dev}, device_id_type=MESH,
+        )
+
+    def site_dev(d):
+        return z * PLANE + fwd(site, d, SITES) * 2 + core
+
+    def z_dev(e):
+        return fwd(z, e, nz) * PLANE + site * 2 + core
+
+    barrier = pltpu.get_barrier_semaphore()
+
+    def greet(d, carry):
+        pl.semaphore_signal(
+            barrier, inc=1, device_id={"ctx": fwd(me, d, n)}, device_id_type=MESH
+        )
+        return carry
+
+    lax.fori_loop(1, n, greet, 0)
+
+    def hin(c):
+        sl = pl.ds(c * cc, cc)
+        return pltpu.make_async_copy(hid_hbm.at[:, sl], hid.at[:, sl], hin_sem.at[c])
+
+    for c in range(CHUNKS):
+        hin(c).start()
+
+    for p in range(pieces):
+        fold32[p * shard_rows:(p + 1) * shard_rows, :] = mst_ref[:, p * cols:(p + 1) * cols]
+    own = slot(core, site, z)
+    wg[own] = fold32[...].astype(bf16)
+    st[me] = stats_ref[...]
+    pl.semaphore_wait(barrier, n - 1)
+
+    def spread(buf, ssem, rsem):
+        def step(d, carry):
+            rcopy(buf.at[me], buf.at[me], ssem.at[d], rsem.at[d], fwd(me, d, n)).start()
+            return carry
+
+        lax.fori_loop(1, n, step, 0)
+
+    def spread_recv(buf, ssem, rsem):
+        def step(d, carry):
+            src = back(me, d, n)
+            rcopy(buf.at[src], buf.at[src], ssem.at[d], rsem.at[d], src).wait_recv()
+            return carry
+
+        lax.fori_loop(1, n, step, 0)
+
+    def spread_sent(buf, ssem, rsem):
+        def step(d, carry):
+            rcopy(buf.at[me], buf.at[me], ssem.at[d], rsem.at[d], fwd(me, d, n)).wait_send()
+            return carry
+
+        lax.fori_loop(1, n, step, 0)
+
+    def zcopy(e, k):
+        ref = wg.at[slot(core, site, k)]
+        return rcopy(ref, ref, zs.at[e], zr.at[e], z_dev(e))
+
+    def pcopy(e, d, s):
+        ref = wg.at[slot(core, s, back(z, e, nz))]
+        return rcopy(ref, ref, ps.at[e, d], pr.at[e, d], site_dev(d))
+
+    def bcopy(e, d, c):
+        ref = wg.at[slot(c, back(site, d, SITES), back(z, e, nz))]
+        return rcopy(ref, ref, bs.at[e, d], br.at[e, d], sib)
+
+    for d in range(1, SITES):
+        pcopy(0, d, site).start()
+    for e in range(1, nz):
+        zcopy(e, z).start()
+    bcopy(0, 0, core).start()
+    spread(st, sts, str_)
+    for e in range(1, nz):
+        zcopy(e, back(z, e, nz)).wait_recv()
+        for d in range(1, SITES):
+            pcopy(e, d, site).start()
+        bcopy(e, 0, core).start()
+    for e in range(nz):
+        for d in range(1, SITES):
+            pcopy(e, d, back(site, d, SITES)).wait_recv()
+            bcopy(e, d, core).start()
+
+    for c in range(CHUNKS):
+        hin(c).wait()
+
+    rb, pb = log2(shard_rows), log2(FOLD)
+    tile = min(512, cols)
+
+    def unfold(h):
+        orow = lax.broadcasted_iota(jnp.int32, (half_rows, FOLD * SITES * nz), 0)
+        icol = lax.broadcasted_iota(jnp.int32, (half_rows, FOLD * SITES * nz), 1)
+        base = ((orow >> rb) << pb) + (orow & (shard_rows - 1))
+        for p in range(pieces):
+            pick = (icol == base + p * shard_rows).astype(f32).astype(bf16)
+
+            def step(t, carry):
+                at = pl.multiple_of(t * tile, tile)
+                got = wg[pl.ds(h * SITES * nz, SITES * nz), :, pl.ds(at, tile)]
+                got = got.reshape(SITES * nz * FOLD, tile)
+                out = jnp.dot(pick, got, preferred_element_type=f32).astype(bf16)
+                w[h, :, pl.ds(pl.multiple_of(p * cols + at, tile), tile)] = out
+                return carry
+
+            lax.fori_loop(0, cols // tile, step, 0)
+
+        def lstep(t, total):
+            sl = pl.ds(pl.multiple_of(t * 1024, 1024), 1024)
+            return total + lax.dot_general(
+                w[h, :, sl], hid[:, sl], (((1,), (1,)), ((), ())), preferred_element_type=f32
+            )
+
+        lg[h] = lax.fori_loop(0, feat // 1024, lstep, jnp.zeros((half_rows, tok), f32))
+
+    unfold(core)
+    for e in range(nz):
+        for d in range(SITES):
+            bcopy(e, d, 1 - core).wait_recv()
+    unfold(1 - core)
+
+    spread_recv(st, sts, str_)
+    picked = []
+    for off in range(2):
+        span = order_ref[2 * me + off]
+        slab = st[lax.div(span, 2)]
+        odd = lax.rem(span, 2)
+        picked.append(
+            [jnp.where(odd == 0, slab[2 * q:2 * q + 1], slab[2 * q + 1:2 * q + 2]) for q in range(4)]
+        )
+    tgt, mask, prior, outside = [
+        jnp.concatenate([picked[0][q], picked[1][q]], axis=1) for q in range(4)
+    ]
+    token_count = jnp.sum(jnp.sum(st[...], axis=0)[2:4])
+    logits = jnp.concatenate([lg[0], lg[1]], axis=0)
+    col = lax.broadcasted_iota(jnp.int32, (group_rows, tok), 0)
+    place = col >> rb
+    zb = log2(nz)
+    home = (place & (nz - 1)) * PLANE + ((place >> zb) & (SITES - 1)) * 2 + (place >> (zb + 2))
+    natural = home * shard_rows + (col & (shard_rows - 1))
+    onehot = (natural.astype(f32) == tgt - float(group_rows)).astype(f32)
+    inside = jnp.sum(logits * onehot, axis=0, keepdims=True)
+    top = jnp.maximum(prior, jnp.max(logits, axis=0, keepdims=True))
+    total = jnp.exp(prior - top) + jnp.sum(jnp.exp(logits - top), axis=0, keepdims=True)
+    log_total = top + jnp.log(total)
+    target_logit = jnp.where(tgt >= float(group_rows), inside, outside)
+    loss = mask * (log_total - target_logit)
+    lb[me] = jnp.concatenate(
+        [loss[:, :half_tok], loss[:, half_tok:], jnp.zeros((6, half_tok), f32)], axis=0
+    )
+    spread(lb, lbs, lbr)
+    scale = loss_scale / jnp.full((1, 1), token_count, f32)
+    dlog = mask * (jnp.exp(logits - log_total) - onehot) * scale
+    dl[0] = dlog[:half_rows].astype(bf16)
+    dl[1] = dlog[half_rows:].astype(bf16)
+    dlt[...] = dlog.T.astype(bf16)
+
+    sub = min(512, cc)
+
+    def grad(h, c, t):
+        sl = pl.ds(pl.multiple_of(c * cc + t * sub, sub), sub)
+        return jnp.dot(dl[h], hid[:, sl], preferred_element_type=f32)
+
+    def tl(t):
+        return pl.ds(pl.multiple_of(t * sub, sub), sub)
+
+    def r0(c):
+        return rcopy(sb0.at[c], rb0.at[c], r0s.at[c], r0r.at[c], sib)
+
+    def r1(c, d):
+        return rcopy(
+            sb1.at[c, fwd(site, d, SITES)], rb1.at[c, d], r1s.at[c, d], r1r.at[c, d], site_dev(d)
+        )
+
+    def r2(c, e):
+        return rcopy(sb2.at[c, fwd(z, e, nz)], rb2.at[c, e], r2s.at[c, e], r2r.at[c, e], z_dev(e))
+
+    for c in range(CHUNKS):
+        def far(t, carry):
+            sb0[c, :, tl(t)] = grad(1 - core, c, t).astype(bf16)
+            return carry
+
+        lax.fori_loop(0, cc // sub, far, 0)
+        r0(c).start()
+    for c in range(CHUNKS):
+        r0(c).wait_recv()
+
+        def near(t, carry):
+            both = grad(core, c, t) + rb0[c, :, tl(t)].astype(f32)
+            both = both.reshape(SITES, half_rows // SITES, sub)
+            acc[c, :, :, tl(t)] = both
+            sb1[c, :, :, tl(t)] = both.astype(bf16)
+            return carry
+
+        lax.fori_loop(0, cc // sub, near, 0)
+        for d in range(1, SITES):
+            r1(c, d).start()
+
+    def hout(c):
+        sl = pl.ds(c * cc, cc)
+        return pltpu.make_async_copy(hg.at[:, sl], hg_hbm.at[:, sl], hout_sem.at[c])
+
+    for c in range(CHUNKS):
+        def back_hidden(t, carry):
+            sl = pl.ds(pl.multiple_of(c * cc + t * sub, sub), sub)
+            rows = jnp.concatenate([w[0, :, sl], w[1, :, sl]], axis=0)
+            hg[:, sl] = jnp.dot(dlt[...], rows, preferred_element_type=f32).astype(bf16)
+            return carry
+
+        lax.fori_loop(0, cc // sub, back_hidden, 0)
+        hout(c).start()
+        for d in range(1, SITES):
+            r1(c, d).wait_recv()
+        both = acc[c, site]
+        for d in range(1, SITES):
+            both = both + rb1[c, d].astype(f32)
+        for k in range(nz):
+            sb2[c, k] = both[k * shard_rows:(k + 1) * shard_rows]
+        for e in range(1, nz):
+            r2(c, e).start()
+    squares = jnp.zeros((shard_rows, cc), f32)
+    for c in range(CHUNKS):
+        g = sb2[c, z]
+        for e in range(1, nz):
+            r2(c, e).wait_recv()
+            g = g + rb2[c, e]
+        gb[:, c * cc:(c + 1) * cc] = g
+        squares = squares + g * g
+    sqb[me] = jnp.full((8, 128), jnp.sum(squares), f32)
+    spread(sqb, sqs, sqr)
+
+    spread_recv(lb, lbs, lbr)
+    ml_ref[...] = jnp.full((1, 1), jnp.sum(lb[...]) / token_count, f32)
+
+    def find(j, carry):
+        here = order_ref[j]
+        a, b = carry
+        return (
+            jnp.where(here == 2 * me, j, a), jnp.where(here == 2 * me + 1, j, b)
+        )
+
+    places = lax.fori_loop(0, 2 * n, find, (jnp.int32(0), jnp.int32(0)))
+    for off in range(2):
+        slab = lb[lax.div(places[off], 2)]
+        odd = lax.rem(places[off], 2)
+        tl_ref[off:off + 1, :] = jnp.where(odd == 0, slab[0:1], slab[1:2])
+
+    spread_recv(sqb, sqs, sqr)
+    norm = jnp.sqrt(jnp.sum(sqb[...], axis=0)[0:1, 0:1]) / loss_scale
+    clip = jnp.minimum(1.0, clip_norm / (norm + 1e-06))
+
+    def adam(t, carry):
+        sl = pl.ds(pl.multiple_of(t * 1024, 1024), 1024)
+        clipped = gb[:, sl] * clip
+        m = beta_one * mom_ref[:, sl] + (1.0 - beta_one) * clipped
+        v = beta_two * sec_ref[:, sl] + (1.0 - beta_two) * clipped * clipped
+        x = mst_ref[:, sl]
+        nmom_ref[:, sl] = m
+        nsec_ref[:, sl] = v
+        nmst_ref[:, sl] = x - learn_rate * (m / (jnp.sqrt(v) + adam_eps) + weight_decay * x)
+        return carry
+
+    lax.fori_loop(0, feat // 1024, adam, 0)
+
+    spread_sent(st, sts, str_)
+    spread_sent(lb, lbs, lbr)
+    spread_sent(sqb, sqs, sqr)
+    for e in range(1, nz):
+        zcopy(e, z).wait_send()
+    for e in range(nz):
+        for d in range(SITES):
+            if d:
+                pcopy(e, d, site).wait_send()
+            bcopy(e, d, core).wait_send()
+    for c in range(CHUNKS):
+        r0(c).wait_send()
+        for d in range(1, SITES):
+            r1(c, d).wait_send()
+        for e in range(1, nz):
+            r2(c, e).wait_send()
+        hout(c).wait()
+
+
+def fused_body(
+    hidden_states, master, moment, second, targets, loss_mask, prior_lse, prior_target, span_order
+):
+    f32, bf16 = jnp.float32, jnp.bfloat16
+    tok, feat = hidden_states.shape
+    shard_rows = master.shape[0]
+    n = lax.axis_size("ctx")
+    nz = n // PLANE
+    half_tok = tok // 2
+    half_rows = shard_rows * SITES * nz
+    cc = feat // CHUNKS
+    stats = jnp.concatenate(
+        [v.astype(f32).reshape(2, half_tok) for v in (targets, loss_mask, prior_lse, prior_target)], 0
+    )
+    dma = pltpu.SemaphoreType.DMA
+    vmem = pl.BlockSpec(memory_space=pltpu.VMEM)
+    smem = pl.BlockSpec(memory_space=pltpu.SMEM)
+    anyw = pl.BlockSpec(memory_space=pl.ANY)
+    out = pl.pallas_call(
+        functools.partial(kernel, n, shard_rows),
+        out_shape=(
+            jax.ShapeDtypeStruct((2, half_tok), f32),
+            jax.ShapeDtypeStruct((1, 1), f32),
+            jax.ShapeDtypeStruct((tok, feat), bf16),
+            jax.ShapeDtypeStruct(master.shape, f32),
+            jax.ShapeDtypeStruct(master.shape, f32),
+            jax.ShapeDtypeStruct(master.shape, f32),
+        ),
+        in_specs=[smem, vmem, vmem, vmem, vmem, anyw],
+        out_specs=(vmem, vmem, anyw, vmem, vmem, vmem),
+        scratch_shapes=[
+            pltpu.VMEM((tok, feat), bf16),
+            pltpu.VMEM((tok, feat), bf16),
+            pltpu.VMEM((FOLD, feat * shard_rows // FOLD), f32),
+            pltpu.VMEM((n, FOLD, feat * shard_rows // FOLD), bf16),
+            pltpu.VMEM((2, half_rows, feat), bf16),
+            pltpu.VMEM((2, half_rows, tok), f32),
+            pltpu.VMEM((2, half_rows, tok), bf16),
+            pltpu.VMEM((tok, 2 * half_rows), bf16),
+            pltpu.VMEM((n, 8, half_tok), f32),
+            pltpu.VMEM((n, 8, half_tok), f32),
+            pltpu.VMEM((n, 8, 128), f32),
+            pltpu.VMEM((CHUNKS, half_rows, cc), bf16),
+            pltpu.VMEM((CHUNKS, half_rows, cc), bf16),
+            pltpu.VMEM((CHUNKS, SITES, half_rows // SITES, cc), f32),
+            pltpu.VMEM((CHUNKS, SITES, half_rows // SITES, cc), bf16),
+            pltpu.VMEM((CHUNKS, SITES, half_rows // SITES, cc), bf16),
+            pltpu.VMEM((CHUNKS, nz, shard_rows, cc), f32),
+            pltpu.VMEM((CHUNKS, nz, shard_rows, cc), f32),
+            pltpu.VMEM((shard_rows, feat), f32),
+            dma((CHUNKS,)), dma((CHUNKS,)),
+            dma((nz,)), dma((nz,)),
+            dma((nz, SITES)), dma((nz, SITES)),
+            dma((nz, SITES)), dma((nz, SITES)),
+            dma((n,)), dma((n,)), dma((n,)), dma((n,)), dma((n,)), dma((n,)),
+            dma((CHUNKS,)), dma((CHUNKS,)),
+            dma((CHUNKS, SITES)), dma((CHUNKS, SITES)),
+            dma((CHUNKS, nz)), dma((CHUNKS, nz)),
+        ],
+        compiler_params=pltpu.CompilerParams(
+            collective_id=0, has_side_effects=True, vmem_limit_bytes=48 * 1024 * 1024
+        ),
+    )(span_order, stats, master, moment, second, hidden_states)
+    token_loss, mean_loss, hidden_grad, new_master, new_moment, new_second = out
+    return (
+        token_loss.reshape(tok), mean_loss.reshape(()), hidden_grad,
+        new_master, new_moment, new_second,
+    )
+
+
 def solution(mesh):
     in_specs = (
         P("ctx", None),
@@ -140,4 +547,6 @@
         P(("vocab", "ctx"), None),
         P(("vocab", "ctx"), None),
     )
+    shape = dict(mesh.shape)
+    body = fused_body if fits(shape) else plain_body
     return jax.shard_map(body, mesh=mesh, in_specs=in_specs, out_specs=out_specs, check_vma=False)

time: 371 us -> 80.5 us (0.22)
  blocking collectives: 233 us -> 0 us
  waiting for transfers between devices: 94.3 us -> 0 us
  Pallas kernels: 0 us -> 63.9 us
  between operations: 20.7 us -> 2.41 us
  matrix products: 9.96 us -> 0 us
  local copies, waits for them, and re-layouts: 4.86 us -> 12.5 us
  other arithmetic: 7.64 us -> 1.4 us
    all_gather x5 -> x0, blocking collectives: 194 us -> none  [the longest x1 43.5 us: body(): lax.all_gather(loss_mask, 'ctx', axis=0, tiled=True)]
    unnamed x3 -> x0, waiting for transfers between devices: 94.3 us -> none
    pallas_call x0 -> x1, Pallas kernels: none -> 63.9 us  [fused_body(): pl.pallas_call(functools.partial(kernel, n, shard_rows), out_shape=(jax.S...]
    psum x1 -> x0, blocking collectives: 39.3 us -> none  [body(): square_sum = lax.psum(jnp.sum(row_grad * row_grad), ('ctx', 'vocab'))]
    dot_general x3 -> x0, matrix products: 9.96 us -> none  [the longest x1 3.95 us: project(): lax.dot_general(block_rows, weight_rows, (((1,), (1,)), ((), ())), prefer...]
    unnamed x11 -> x15, local copies, waits for them, and re-layouts: 3.15 us -> 12.5 us
  transfers between devices with their start and end apart: 2 -> 0, of which waited for: 1 -> 0; matrix products, arithmetic and copies ran while one was open for 2% -> 0% of each run, Pallas kernels for 0% -> 0%
where the time goes in v1:
time: 80.5 us; the launch traced here: 80.2 us
  Pallas kernels  63.9 us (79%)
  local copies, waits for them, and re-layouts  12.5 us (16%)
  between operations  2.41 us (3%)
  other arithmetic  1.4 us (2%)
    pallas_call x1, Pallas kernels, fused_body(): pl.pallas_call(functools.partial(kernel, n, shard_rows), out_shape=(jax.S...  63.9 us
    unnamed x15, local copies, waits for them, and re-layouts  12.5 us

profile of v1, /device:TPU:0, one launch (start us, length us, event | category | flops | bytes accessed | tf_op | source)
XLA Modules:
  0.0 80.2 jit_solution(13846888080544602391)
XLA Ops:
  0.6 0.7 convert_bitcast_fusion
  1.3 0.7 pad_maximum_fusion.stats_ref
  2.0 0.0 copy-start.1
  2.0 0.9 %copy-done.1 = f32[4,8192]{1,0:T(4,128)S(1)} copy-done((f32[4,8192]{1,0:T(4,128)S(1)}, f32[4,8192]{1,0:T(4,128)}, u32[]{:S(2)}) %copy-start.1) | copy-done | bytes 131096
  2.9 0.0 copy-start.2
  2.9 0.9 %copy-done.2 = f32[4,8192]{1,0:T(4,128)S(1)} copy-done((f32[4,8192]{1,0:T(4,128)S(1)}, f32[4,8192]{1,0:T(4,128)}, u32[]{:S(2)}) %copy-start.2) | copy-done | bytes 131096
  3.8 0.0 copy-start.3
  3.8 0.9 %copy-done.3 = f32[4,8192]{1,0:T(4,128)S(1)} copy-done((f32[4,8192]{1,0:T(4,128)S(1)}, f32[4,8192]{1,0:T(4,128)}, u32[]{:S(2)}) %copy-start.3) | copy-done | bytes 131096
  4.8 0.0 copy-start.4
  4.8 0.7 copy-done.4
  5.4 63.9 %shard_map.136 = (f32[2,128]{1,0:T(2,128)S(1)}, f32[1,1]{1,0:T(1,128)}, bf16[256,8192]{1,0:T(8,128)(2,1)S(1)}, f32[4,8192]{1,0:T(4,128)S(1)}, f32[4,8192]{1,0:T(4,128)S(1)}, /*index=5*/f32[4,8192]{1,0:T(4,128)S(1)}) custom-call(s32[64]{0:T(128)S(1)} %copy-done.4, f32[8,128]{1,0:T(8,128)S(1)} %pad_maximum_fusion.stats_ref, f32[4,8192]{1,0:T(4,128)S(1)} %copy-done.1, ...), custom_call_target="tpu_custom_call" | custom-call | tf_op jit(solution)/shard_map/pallas_call | solution.py:478
  69.4 0.0 copy-start
  69.4 1.9 %copy-done = bf16[256,8192]{1,0:T(8,128)(2,1)} copy-done((bf16[256,8192]{1,0:T(8,128)(2,1)}, bf16[256,8192]{1,0:T(8,128)(2,1)S(1)}, u32[]{:S(2)}) %copy-start) | copy-done | bytes 4194328
  71.3 0.6 copy.21
  72.5 4.6 %copy.23 = bf16[256,8192]{1,0:T(8,128)(2,1)} copy(bf16[256,8192]{1,0:T(8,128)(2,1)} %copy-done) | data formatting | bytes 8388608
  77.1 0.7 copy.24
  77.8 0.7 copy.25
  78.4 0.7 copy.26
Async XLA Ops:
  2.0 0.9 %copy-start.1 = (f32[4,8192]{1,0:T(4,128)S(1)}, f32[4,8192]{1,0:T(4,128)}, u32[]{:S(2)}) copy-start(f32[4,8192]{1,0:T(4,128)} %mst_ref.1) | copy-start | bytes 393220
  2.9 0.9 %copy-start.2 = (f32[4,8192]{1,0:T(4,128)S(1)}, f32[4,8192]{1,0:T(4,128)}, u32[]{:S(2)}) copy-start(f32[4,8192]{1,0:T(4,128)} %mom_ref.1) | copy-start | bytes 393220
  3.8 0.9 %copy-start.3 = (f32[4,8192]{1,0:T(4,128)S(1)}, f32[4,8192]{1,0:T(4,128)}, u32[]{:S(2)}) copy-start(f32[4,8192]{1,0:T(4,128)} %sec_ref.1) | copy-start | bytes 393220
  4.8 0.7 copy-start.4
  69.4 1.9 %copy-start = (bf16[256,8192]{1,0:T(8,128)(2,1)}, bf16[256,8192]{1,0:T(8,128)(2,1)S(1)}, u32[]{:S(2)}) copy-start(bf16[256,8192]{1,0:T(8,128)(2,1)S(1)} %get-tuple-element.28) | copy-start | bytes 12582916

commit v2 on v1

--- a/solution.py
+++ b/solution.py
@@ -129,6 +129,7 @@
 SITES = 4
 FOLD = 16
 CHUNKS = 4
+PARTS = 2
 
 
 def fits(shape):
@@ -141,10 +142,10 @@
 
 
 def kernel(
-    n, shard_rows, order_ref, stats_ref, mst_ref, mom_ref, sec_ref, hid_hbm,
-    tl_ref, ml_ref, hg_hbm, nmst_ref, nmom_ref, nsec_ref,
-    hid, hg, fold32, wg, w, lg, dl, dlt, st, lb, sqb, sb0, rb0, acc, sb1, rb1, sb2, rb2, gb,
-    hin_sem, hout_sem, zs, zr, ps, pr, bs, br, sts, str_, lbs, lbr, sqs, sqr,
+    n, shard_rows, order_hbm, stats_ref, mst_hbm, hid_hbm,
+    tl_ref, ml_ref, w, dlt, gb, sq_ref,
+    order_ref, mst_ref, hid, fold32, wg, lg, dl, st, lb, sqb, sb0, rb0, acc, sb1, rb1, sb2, rb2,
+    in_sem, hin_sem, zs, zr, ps, pr, bs, br, sts, str_, lbs, lbr, sqs, sqr,
     r0s, r0r, r1s, r1r, r2s, r2r,
 ):
     f32, bf16 = jnp.float32, jnp.bfloat16
@@ -155,6 +156,7 @@
     pieces = FOLD // shard_rows
     cols = feat // pieces
     cc = feat // CHUNKS
+    gc = cols // PARTS
     half_rows = shard_rows * SITES * nz
     group_rows = 2 * half_rows
     me = lax.axis_index("ctx")
@@ -198,13 +200,19 @@
         sl = pl.ds(c * cc, cc)
         return pltpu.make_async_copy(hid_hbm.at[:, sl], hid.at[:, sl], hin_sem.at[c])
 
+    mst_in = pltpu.make_async_copy(mst_hbm, mst_ref, in_sem.at[0])
+    order_in = pltpu.make_async_copy(order_hbm, order_ref, in_sem.at[1])
+    mst_in.start()
+    order_in.start()
     for c in range(CHUNKS):
         hin(c).start()
+    mst_in.wait()
 
     for p in range(pieces):
         fold32[p * shard_rows:(p + 1) * shard_rows, :] = mst_ref[:, p * cols:(p + 1) * cols]
     own = slot(core, site, z)
-    wg[own] = fold32[...].astype(bf16)
+    for g in range(PARTS):
+        wg[g, own] = fold32[:, g * gc:(g + 1) * gc].astype(bf16)
     st[me] = stats_ref[...]
     pl.semaphore_wait(barrier, n - 1)
 
@@ -230,71 +238,72 @@
 
         lax.fori_loop(1, n, step, 0)
 
-    def zcopy(e, k):
-        ref = wg.at[slot(core, site, k)]
-        return rcopy(ref, ref, zs.at[e], zr.at[e], z_dev(e))
-
-    def pcopy(e, d, s):
-        ref = wg.at[slot(core, s, back(z, e, nz))]
-        return rcopy(ref, ref, ps.at[e, d], pr.at[e, d], site_dev(d))
-
-    def bcopy(e, d, c):
-        ref = wg.at[slot(c, back(site, d, SITES), back(z, e, nz))]
-        return rcopy(ref, ref, bs.at[e, d], br.at[e, d], sib)
-
-    for d in range(1, SITES):
-        pcopy(0, d, site).start()
-    for e in range(1, nz):
-        zcopy(e, z).start()
-    bcopy(0, 0, core).start()
+    def zcopy(g, e, k):
+        ref = wg.at[g, slot(core, site, k)]
+        return rcopy(ref, ref, zs.at[g, e], zr.at[g, e], z_dev(e))
+
+    def pcopy(g, e, d, s):
+        ref = wg.at[g, slot(core, s, back(z, e, nz))]
+        return rcopy(ref, ref, ps.at[g, e, d], pr.at[g, e, d], site_dev(d))
+
+    def bcopy(g, e, d, c):
+        ref = wg.at[g, slot(c, back(site, d, SITES), back(z, e, nz))]
+        return rcopy(ref, ref, bs.at[g, e, d], br.at[g, e, d], sib)
+
+    for g in range(PARTS):
+        for d in range(1, SITES):
+            pcopy(g, 0, d, site).start()
+        for e in range(1, nz):
+            zcopy(g, e, z).start()
+        bcopy(g, 0, 0, core).start()
     spread(st, sts, str_)
-    for e in range(1, nz):
-        zcopy(e, back(z, e, nz)).wait_recv()
-        for d in range(1, SITES):
-            pcopy(e, d, site).start()
-        bcopy(e, 0, core).start()
-    for e in range(nz):
-        for d in range(1, SITES):
-            pcopy(e, d, back(site, d, SITES)).wait_recv()
-            bcopy(e, d, core).start()
-
-    for c in range(CHUNKS):
-        hin(c).wait()
+    for g in range(PARTS):
+        for e in range(1, nz):
+            zcopy(g, e, back(z, e, nz)).wait_recv()
+            for d in range(1, SITES):
+                pcopy(g, e, d, site).start()
+            bcopy(g, e, 0, core).start()
 
     rb, pb = log2(shard_rows), log2(FOLD)
-    tile = min(512, cols)
-
-    def unfold(h):
-        orow = lax.broadcasted_iota(jnp.int32, (half_rows, FOLD * SITES * nz), 0)
-        icol = lax.broadcasted_iota(jnp.int32, (half_rows, FOLD * SITES * nz), 1)
-        base = ((orow >> rb) << pb) + (orow & (shard_rows - 1))
-        for p in range(pieces):
-            pick = (icol == base + p * shard_rows).astype(f32).astype(bf16)
-
-            def step(t, carry):
-                at = pl.multiple_of(t * tile, tile)
-                got = wg[pl.ds(h * SITES * nz, SITES * nz), :, pl.ds(at, tile)]
-                got = got.reshape(SITES * nz * FOLD, tile)
-                out = jnp.dot(pick, got, preferred_element_type=f32).astype(bf16)
-                w[h, :, pl.ds(pl.multiple_of(p * cols + at, tile), tile)] = out
-                return carry
-
-            lax.fori_loop(0, cols // tile, step, 0)
-
-        def lstep(t, total):
-            sl = pl.ds(pl.multiple_of(t * 1024, 1024), 1024)
-            return total + lax.dot_general(
-                w[h, :, sl], hid[:, sl], (((1,), (1,)), ((), ())), preferred_element_type=f32
-            )
-
-        lg[h] = lax.fori_loop(0, feat // 1024, lstep, jnp.zeros((half_rows, tok), f32))
-
-    unfold(core)
-    for e in range(nz):
-        for d in range(SITES):
-            bcopy(e, d, 1 - core).wait_recv()
-    unfold(1 - core)
-
+    orow = lax.broadcasted_iota(jnp.int32, (half_rows, FOLD * SITES * nz), 0)
+    icol = lax.broadcasted_iota(jnp.int32, (half_rows, FOLD * SITES * nz), 1)
+    base = ((orow >> rb) << pb) + (orow & (shard_rows - 1))
+
+    def unfold(g, p):
+        pick = (icol == base + p * shard_rows).astype(f32).astype(bf16)
+        lo = p * cols + g * gc
+        for h in range(2):
+            got = wg[g, h * SITES * nz:(h + 1) * SITES * nz]
+            got = got.reshape(SITES * nz * FOLD, gc)
+            out = jnp.dot(pick, got, preferred_element_type=f32).astype(bf16)
+            w[h * half_rows:(h + 1) * half_rows, lo:lo + gc] = out
+        part = lax.dot_general(
+            w[:, lo:lo + gc], hid[:, lo:lo + gc], (((1,), (1,)), ((), ())),
+            preferred_element_type=f32,
+        )
+        if g == 0 and p == 0:
+            lg[...] = part
+        else:
+            lg[...] += part
+
+    for g in range(PARTS):
+        for e in range(nz):
+            for d in range(1, SITES):
+                pcopy(g, e, d, back(site, d, SITES)).wait_recv()
+                bcopy(g, e, d, core).start()
+            if g:
+                for p in range(e, pieces, nz):
+                    unfold(g - 1, p)
+        if g == 0:
+            for c in range(CHUNKS):
+                hin(c).wait()
+        for e in range(nz):
+            for d in range(SITES):
+                bcopy(g, e, d, 1 - core).wait_recv()
+    for p in range(pieces):
+        unfold(PARTS - 1, p)
+
+    order_in.wait()
     spread_recv(st, sts, str_)
     picked = []
     for off in range(2):
@@ -308,7 +317,7 @@
         jnp.concatenate([picked[0][q], picked[1][q]], axis=1) for q in range(4)
     ]
     token_count = jnp.sum(jnp.sum(st[...], axis=0)[2:4])
-    logits = jnp.concatenate([lg[0], lg[1]], axis=0)
+    logits = lg[...]
     col = lax.broadcasted_iota(jnp.int32, (group_rows, tok), 0)
     place = col >> rb
     zb = log2(nz)
@@ -372,19 +381,7 @@
         for d in range(1, SITES):
             r1(c, d).start()
 
-    def hout(c):
-        sl = pl.ds(c * cc, cc)
-        return pltpu.make_async_copy(hg.at[:, sl], hg_hbm.at[:, sl], hout_sem.at[c])
-
     for c in range(CHUNKS):
-        def back_hidden(t, carry):
-            sl = pl.ds(pl.multiple_of(c * cc + t * sub, sub), sub)
-            rows = jnp.concatenate([w[0, :, sl], w[1, :, sl]], axis=0)
-            hg[:, sl] = jnp.dot(dlt[...], rows, preferred_element_type=f32).astype(bf16)
-            return carry
-
-        lax.fori_loop(0, cc // sub, back_hidden, 0)
-        hout(c).start()
         for d in range(1, SITES):
             r1(c, d).wait_recv()
         both = acc[c, site]
@@ -422,39 +419,25 @@
         tl_ref[off:off + 1, :] = jnp.where(odd == 0, slab[0:1], slab[1:2])
 
     spread_recv(sqb, sqs, sqr)
-    norm = jnp.sqrt(jnp.sum(sqb[...], axis=0)[0:1, 0:1]) / loss_scale
-    clip = jnp.minimum(1.0, clip_norm / (norm + 1e-06))
-
-    def adam(t, carry):
-        sl = pl.ds(pl.multiple_of(t * 1024, 1024), 1024)
-        clipped = gb[:, sl] * clip
-        m = beta_one * mom_ref[:, sl] + (1.0 - beta_one) * clipped
-        v = beta_two * sec_ref[:, sl] + (1.0 - beta_two) * clipped * clipped
-        x = mst_ref[:, sl]
-        nmom_ref[:, sl] = m
-        nsec_ref[:, sl] = v
-        nmst_ref[:, sl] = x - learn_rate * (m / (jnp.sqrt(v) + adam_eps) + weight_decay * x)
-        return carry
-
-    lax.fori_loop(0, feat // 1024, adam, 0)
+    sq_ref[...] = jnp.sum(sqb[...], axis=0)[0:1, 0:1]
 
     spread_sent(st, sts, str_)
     spread_sent(lb, lbs, lbr)
     spread_sent(sqb, sqs, sqr)
-    for e in range(1, nz):
-        zcopy(e, z).wait_send()
-    for e in range(nz):
-        for d in range(SITES):
-            if d:
-                pcopy(e, d, site).wait_send()
-            bcopy(e, d, core).wait_send()
+    for g in range(PARTS):
+        for e in range(1, nz):
+            zcopy(g, e, z).wait_send()
+        for e in range(nz):
+            for d in range(SITES):
+                if d:
+                    pcopy(g, e, d, site).wait_send()
+                bcopy(g, e, d, core).wait_send()
     for c in range(CHUNKS):
         r0(c).wait_send()
         for d in range(1, SITES):
             r1(c, d).wait_send()
         for e in range(1, nz):
             r2(c, e).wait_send()
-        hout(c).wait()
 
 
 def fused_body(
@@ -473,29 +456,28 @@
     )
     dma = pltpu.SemaphoreType.DMA
     vmem = pl.BlockSpec(memory_space=pltpu.VMEM)
-    smem = pl.BlockSpec(memory_space=pltpu.SMEM)
-    anyw = pl.BlockSpec(memory_space=pl.ANY)
+    hbm = pl.BlockSpec(memory_space=pltpu.HBM)
+    gc = feat * shard_rows // FOLD // PARTS
     out = pl.pallas_call(
         functools.partial(kernel, n, shard_rows),
         out_shape=(
             jax.ShapeDtypeStruct((2, half_tok), f32),
             jax.ShapeDtypeStruct((1, 1), f32),
-            jax.ShapeDtypeStruct((tok, feat), bf16),
+            jax.ShapeDtypeStruct((2 * half_rows, feat), bf16),
+            jax.ShapeDtypeStruct((tok, 2 * half_rows), bf16),
             jax.ShapeDtypeStruct(master.shape, f32),
-            jax.ShapeDtypeStruct(master.shape, f32),
-            jax.ShapeDtypeStruct(master.shape, f32),
+            jax.ShapeDtypeStruct((1, 1), f32),
         ),
-        in_specs=[smem, vmem, vmem, vmem, vmem, anyw],
-        out_specs=(vmem, vmem, anyw, vmem, vmem, vmem),
+        in_specs=[hbm, vmem, hbm, hbm],
+        out_specs=(vmem, vmem, vmem, vmem, vmem, vmem),
         scratch_shapes=[
-            pltpu.VMEM((tok, feat), bf16),
+            pltpu.SMEM(span_order.shape, jnp.int32),
+            pltpu.VMEM(master.shape, f32),
             pltpu.VMEM((tok, feat), bf16),
             pltpu.VMEM((FOLD, feat * shard_rows // FOLD), f32),
-            pltpu.VMEM((n, FOLD, feat * shard_rows // FOLD), bf16),
-            pltpu.VMEM((2, half_rows, feat), bf16),
-            pltpu.VMEM((2, half_rows, tok), f32),
+            pltpu.VMEM((PARTS, n, FOLD, gc), bf16),
+            pltpu.VMEM((2 * half_rows, tok), f32),
             pltpu.VMEM((2, half_rows, tok), bf16),
-            pltpu.VMEM((tok, 2 * half_rows), bf16),
             pltpu.VMEM((n, 8, half_tok), f32),
             pltpu.VMEM((n, 8, half_tok), f32),
             pltpu.VMEM((n, 8, 128), f32),
@@ -506,11 +488,10 @@
             pltpu.VMEM((CHUNKS, SITES, half_rows // SITES, cc), bf16),
             pltpu.VMEM((CHUNKS, nz, shard_rows, cc), f32),
             pltpu.VMEM((CHUNKS, nz, shard_rows, cc), f32),
-            pltpu.VMEM((shard_rows, feat), f32),
-            dma((CHUNKS,)), dma((CHUNKS,)),
-            dma((nz,)), dma((nz,)),
-            dma((nz, SITES)), dma((nz, SITES)),
-            dma((nz, SITES)), dma((nz, SITES)),
+            dma((2,)), dma((CHUNKS,)),
+            dma((PARTS, nz)), dma((PARTS, nz)),
+            dma((PARTS, nz, SITES)), dma((PARTS, nz, SITES)),
+            dma((PARTS, nz, SITES)), dma((PARTS, nz, SITES)),
             dma((n,)), dma((n,)), dma((n,)), dma((n,)), dma((n,)), dma((n,)),
             dma((CHUNKS,)), dma((CHUNKS,)),
             dma((CHUNKS, SITES)), dma((CHUNKS, SITES)),
@@ -519,8 +500,17 @@
         compiler_params=pltpu.CompilerParams(
             collective_id=0, has_side_effects=True, vmem_limit_bytes=48 * 1024 * 1024
         ),
-    )(span_order, stats, master, moment, second, hidden_states)
-    token_loss, mean_loss, hidden_grad, new_master, new_moment, new_second = out
+    )(span_order, stats, master, hidden_states)
+    token_loss, mean_loss, rows, dlogits, row_grad, square_sum = out
+    hidden_grad = jnp.dot(dlogits, rows, preferred_element_type=f32).astype(bf16)
+    norm_value = jnp.sqrt(square_sum) / loss_scale
+    clip_factor = jnp.minimum(1.0, clip_norm / (norm_value + 1e-06))
+    clipped = row_grad * clip_factor
+    new_moment = beta_one * moment + (1.0 - beta_one) * clipped
+    new_second = beta_two * second + (1.0 - beta_two) * clipped * clipped
+    new_master = master - learn_rate * (
+        new_moment / (jnp.sqrt(new_second) + adam_eps) + weight_decay * master
+    )
     return (
         token_loss.reshape(tok), mean_loss.reshape(()), hidden_grad,
         new_master, new_moment, new_second,

time: 80.5 us -> 67.7 us (0.84)
  local copies, waits for them, and re-layouts: 12.5 us -> 2.13 us
  Pallas kernels: 63.9 us -> 56.6 us
  matrix products: 0 us -> 3.26 us
  other arithmetic: 1.4 us -> 2.32 us
    unnamed x15 -> x9, local copies, waits for them, and re-layouts: 12.5 us -> 2.13 us
    pallas_call x1, Pallas kernels: 63.9 us -> 56.6 us  [fused_body(): pl.pallas_call(functools.partial(kernel, n, shard_rows), out_shape=(jax.S...]
    dot_general x0 -> x1, matrix products: none -> 3.26 us  [fused_body(): jnp.dot(dlogits, rows, preferred_element_type=f32).astype(bf16)]
    sub x0 -> x1, other arithmetic: none -> 0.91 us  [fused_body(): master - learn_rate * (new_moment / (jnp.sqrt(new_second) + adam_eps) + w...]
where the time goes in v2:
time: 67.7 us; the launch traced here: 67.5 us
  Pallas kernels  56.6 us (84%)
  matrix products  3.26 us (5%)
  between operations  3.15 us (5%)
  other arithmetic  2.32 us (3%)
  local copies, waits for them, and re-layouts  2.13 us (3%)
    pallas_call x1, Pallas kernels, fused_body(): pl.pallas_call(functools.partial(kernel, n, shard_rows), out_shape=(jax.S...  56.6 us
    dot_general x1, matrix products, fused_body(): jnp.dot(dlogits, rows, preferred_element_type=f32).astype(bf16)  3.26 us
    unnamed x9, local copies, waits for them, and re-layouts  2.13 us

profile of v2, /device:TPU:0, one launch (start us, length us, event | category | flops | bytes accessed | tf_op | source)
XLA Modules:
  0.0 67.5 jit_solution(5711639489541301606)
XLA Ops:
  0.6 0.7 %convert_bitcast_fusion = (f32[2,128]{1,0:T(2,128)S(1)}, f32[2,128]{1,0:T(2,128)S(1)}) fusion(s32[256]{0:T(256)} %param.14, s32[256]{0:T(256)} %param.13), kind=kLoop, calls=%fused_computation.6 | loop fusion | flops 512 | bytes 4096 | tf_op jit(solution)/shard_map/reshape | solution.py:455
  1.3 0.7 %pad_maximum_fusion.stats_ref = f32[8,128]{1,0:T(8,128)S(1)} fusion(f32[2,128]{1,0:T(2,128)} %bitcast.12, f32[2,128]{1,0:T(2,128)} %bitcast.13, f32[2,128]{1,0:T(2,128)S(1)} %get-tuple-element.21, f32[2,128]{1,0:T(2,128)S(1)} %get-tuple-element.22), kind=kLoop, calls=%fused_computation.5 | loop fusion | flops 3072 | bytes 8192 | tf_op jit(solution)/shard_map/concatenate | solution.py:454
  2.0 0.0 copy-start
  2.0 0.9 %copy-done = f32[4,8192]{1,0:T(4,128)S(1)} copy-done((f32[4,8192]{1,0:T(4,128)S(1)}, f32[4,8192]{1,0:T(4,128)}, u32[]{:S(2)}) %copy-start) | copy-done | bytes 131096
  2.9 0.0 copy-start.1
  3.0 0.7 copy-done.1
  3.6 56.6 %shard_map.136 = (f32[2,128]{1,0:T(2,128)S(1)}, f32[1,1]{1,0:T(1,128)}, bf16[128,8192]{1,0:T(8,128)(2,1)S(1)}, bf16[256,128]{1,0:T(8,128)(2,1)S(1)}, f32[4,8192]{1,0:T(4,128)S(1)}, /*index=5*/f32[1,1]{1,0:T(1,128)}) custom-call(s32[64]{0:T(128)S(1)} %copy-done.1, f32[8,128]{1,0:T(8,128)S(1)} %pad_maximum_fusion.stats_ref, f32[4,8192]{1,0:T(4,128)S(1)} %copy-done, ...), custom_call_target="tpu_custom_call" | custom-call | tf_op jit(solution)/shard_map/pallas_call | solution.py:461
  60.2 0.0 copy-start.2
  60.3 0.0 copy-start.3
  60.3 3.3 %convolution_convert_fusion = bf16[256,8192]{1,0:T(8,128)(2,1)} fusion(bf16[256,128]{1,0:T(8,128)(2,1)S(1)} %get-tuple-element.14, bf16[128,8192]{1,0:T(8,128)(2,1)S(1)} %get-tuple-element.15), kind=kOutput, calls=%fused_computation | convolution fusion | flops 538968064 | bytes 6356992 | tf_op jit(solution)/shard_map/dot_general | solution.py:505
  64.2 0.0 copy-done.2
  64.2 0.0 copy-done.3
  64.2 0.9 %multiply_subtract_fusion = (f32[4,8192]{1,0:T(4,128)}, f32[4,8192]{1,0:T(4,128)}, f32[4,8192]{1,0:T(4,128)}) fusion(f32[4,8192]{1,0:T(4,128)S(1)} %copy-done, f32[4,8192]{1,0:T(4,128)S(1)} %get-tuple-element.16, f32[]{:T(128)} %bitcast.6, f32[4,8192]{1,0:T(4,128)S(1)} %copy-done.2, f32[4,8192]{1,0:T(4,128)S(1)} %copy-done.3), kind=kLoop, calls=%fused_computation.3 | loop fusion | flops 458752 | bytes 917508 | tf_op jit(solution)/shard_map/sub | solution.py:511
  65.1 0.6 copy.17
Async XLA Ops:
  2.0 0.9 %copy-start = (f32[4,8192]{1,0:T(4,128)S(1)}, f32[4,8192]{1,0:T(4,128)}, u32[]{:S(2)}) copy-start(f32[4,8192]{1,0:T(4,128)} %mst_hbm.1) | copy-start | bytes 393220
  2.9 0.7 copy-start.1
  60.2 3.9 %copy-start.2 = (f32[4,8192]{1,0:T(4,128)S(1)}, f32[4,8192]{1,0:T(4,128)}, u32[]{:S(2)}) copy-start(f32[4,8192]{1,0:T(4,128)} %param.12) | copy-start | bytes 393220
  60.3 3.9 %copy-start.3 = (f32[4,8192]{1,0:T(4,128)S(1)}, f32[4,8192]{1,0:T(4,128)}, u32[]{:S(2)}) copy-start(f32[4,8192]{1,0:T(4,128)} %param.11) | copy-start | bytes 393220

commit v3 on v2

--- a/solution.py
+++ b/solution.py
@@ -128,7 +128,7 @@
 PLANE = 8
 SITES = 4
 FOLD = 16
-CHUNKS = 4
+CHUNKS = 8
 PARTS = 2
 
 
@@ -144,8 +144,8 @@
 def kernel(
     n, shard_rows, order_hbm, stats_ref, mst_hbm, hid_hbm,
     tl_ref, ml_ref, w, dlt, gb, sq_ref,
-    order_ref, mst_ref, hid, fold32, wg, lg, dl, st, lb, sqb, sb0, rb0, acc, sb1, rb1, sb2, rb2,
-    in_sem, hin_sem, zs, zr, ps, pr, bs, br, sts, str_, lbs, lbr, sqs, sqr,
+    order_ref, mst_ref, hid, fold32, wg, lg, dl, st, lb, sqa, sqb, sb0, rb0, acc, sb1, rb1, sb2, rb2,
+    in_sem, hin_sem, zs, zr, ps, pr, bs, br, st_sem, lb_sem, sq_sem,
     r0s, r0r, r1s, r1r, r2s, r2r,
 ):
     f32, bf16 = jnp.float32, jnp.bfloat16
@@ -188,13 +188,9 @@
 
     barrier = pltpu.get_barrier_semaphore()
 
-    def greet(d, carry):
-        pl.semaphore_signal(
-            barrier, inc=1, device_id={"ctx": fwd(me, d, n)}, device_id_type=MESH
-        )
-        return carry
-
-    lax.fori_loop(1, n, greet, 0)
+    partners = [sib] + [site_dev(d) for d in range(1, SITES)] + [z_dev(e) for e in range(1, nz)]
+    for dev in partners:
+        pl.semaphore_signal(barrier, inc=1, device_id={"ctx": dev}, device_id_type=MESH)
 
     def hin(c):
         sl = pl.ds(c * cc, cc)
@@ -213,30 +209,45 @@
     own = slot(core, site, z)
     for g in range(PARTS):
         wg[g, own] = fold32[:, g * gc:(g + 1) * gc].astype(bf16)
-    st[me] = stats_ref[...]
-    pl.semaphore_wait(barrier, n - 1)
-
-    def spread(buf, ssem, rsem):
-        def step(d, carry):
-            rcopy(buf.at[me], buf.at[me], ssem.at[d], rsem.at[d], fwd(me, d, n)).start()
-            return carry
-
-        lax.fori_loop(1, n, step, 0)
-
-    def spread_recv(buf, ssem, rsem):
-        def step(d, carry):
-            src = back(me, d, n)
-            rcopy(buf.at[src], buf.at[src], ssem.at[d], rsem.at[d], src).wait_recv()
-            return carry
-
-        lax.fori_loop(1, n, step, 0)
-
-    def spread_sent(buf, ssem, rsem):
-        def step(d, carry):
-            rcopy(buf.at[me], buf.at[me], ssem.at[d], rsem.at[d], fwd(me, d, n)).wait_send()
-            return carry
-
-        lax.fori_loop(1, n, step, 0)
+    st[own] = stats_ref[...]
+    pl.semaphore_wait(barrier, len(partners))
+
+    def zbulk(buf, sems, e, k):
+        ref = buf.at[slot(core, site, k)]
+        return rcopy(ref, ref, sems.at[0, e], sems.at[1, e], z_dev(e))
+
+    def pbulk(buf, sems, d, s):
+        ref = buf.at[pl.ds(slot(core, s, 0), nz)]
+        return rcopy(ref, ref, sems.at[0, nz + d], sems.at[1, nz + d], site_dev(d))
+
+    def bbulk(buf, sems, c):
+        ref = buf.at[pl.ds(c * SITES * nz, SITES * nz)]
+        return rcopy(ref, ref, sems.at[0, 0], sems.at[1, 0], sib)
+
+    def first(buf, sems):
+        for e in range(1, nz):
+            zbulk(buf, sems, e, z).start()
+
+    def second(buf, sems):
+        for e in range(1, nz):
+            zbulk(buf, sems, e, back(z, e, nz)).wait_recv()
+        for d in range(1, SITES):
+            pbulk(buf, sems, d, site).start()
+
+    def third(buf, sems):
+        for d in range(1, SITES):
+            pbulk(buf, sems, d, back(site, d, SITES)).wait_recv()
+        bbulk(buf, sems, core).start()
+
+    def bulk_sent(buf, sems):
+        for e in range(1, nz):
+            zbulk(buf, sems, e, z).wait_send()
+        for d in range(1, SITES):
+            pbulk(buf, sems, d, site).wait_send()
+        bbulk(buf, sems, core).wait_send()
+
+    def device_slot(dev):
+        return slot(lax.rem(dev, 2), lax.rem(lax.div(dev, 2), SITES), lax.div(dev, PLANE))
 
     def zcopy(g, e, k):
         ref = wg.at[g, slot(core, site, k)]
@@ -256,8 +267,10 @@
         for e in range(1, nz):
             zcopy(g, e, z).start()
         bcopy(g, 0, 0, core).start()
-    spread(st, sts, str_)
+    first(st, st_sem)
     for g in range(PARTS):
+        if g == PARTS - 1:
+            second(st, st_sem)
         for e in range(1, nz):
             zcopy(g, e, back(z, e, nz)).wait_recv()
             for d in range(1, SITES):
@@ -295,6 +308,7 @@
                 for p in range(e, pieces, nz):
                     unfold(g - 1, p)
         if g == 0:
+            third(st, st_sem)
             for c in range(CHUNKS):
                 hin(c).wait()
         for e in range(nz):
@@ -304,11 +318,11 @@
         unfold(PARTS - 1, p)
 
     order_in.wait()
-    spread_recv(st, sts, str_)
+    bbulk(st, st_sem, 1 - core).wait_recv()
     picked = []
     for off in range(2):
         span = order_ref[2 * me + off]
-        slab = st[lax.div(span, 2)]
+        slab = st[device_slot(lax.div(span, 2))]
         odd = lax.rem(span, 2)
         picked.append(
             [jnp.where(odd == 0, slab[2 * q:2 * q + 1], slab[2 * q + 1:2 * q + 2]) for q in range(4)]
@@ -330,10 +344,10 @@
     log_total = top + jnp.log(total)
     target_logit = jnp.where(tgt >= float(group_rows), inside, outside)
     loss = mask * (log_total - target_logit)
-    lb[me] = jnp.concatenate(
+    lb[own] = jnp.concatenate(
         [loss[:, :half_tok], loss[:, half_tok:], jnp.zeros((6, half_tok), f32)], axis=0
     )
-    spread(lb, lbs, lbr)
+    first(lb, lb_sem)
     scale = loss_scale / jnp.full((1, 1), token_count, f32)
     dlog = mask * (jnp.exp(logits - log_total) - onehot) * scale
     dl[0] = dlog[:half_rows].astype(bf16)
@@ -367,6 +381,7 @@
 
         lax.fori_loop(0, cc // sub, far, 0)
         r0(c).start()
+    second(lb, lb_sem)
     for c in range(CHUNKS):
         r0(c).wait_recv()
 
@@ -380,6 +395,7 @@
         lax.fori_loop(0, cc // sub, near, 0)
         for d in range(1, SITES):
             r1(c, d).start()
+    third(lb, lb_sem)
 
     for c in range(CHUNKS):
         for d in range(1, SITES):
@@ -399,10 +415,27 @@
             g = g + rb2[c, e]
         gb[:, c * cc:(c + 1) * cc] = g
         squares = squares + g * g
-    sqb[me] = jnp.full((8, 128), jnp.sum(squares), f32)
-    spread(sqb, sqs, sqr)
-
-    spread_recv(lb, lbs, lbr)
+    def hop(src, dst, dev):
+        return rcopy(sqa.at[src], sqb.at[dst], sq_sem.at[0, dst], sq_sem.at[1, dst], dev)
+
+    def hop_sum(value, src, hops):
+        sqa[src] = value
+        for dst, dev in hops:
+            hop(src, dst, dev).start()
+        return value, src, hops
+
+    def hop_done(value, src, hops):
+        for dst, dev in hops:
+            hop(src, dst, dev).wait_recv()
+            value = value + sqb[dst]
+        return value
+
+    by_core = [(0, sib)]
+    by_site = [(d, site_dev(d)) for d in range(1, SITES)]
+    by_z = [(SITES - 1 + e, z_dev(e)) for e in range(1, nz)]
+    pending = hop_sum(jnp.full((8, 128), jnp.sum(squares), f32), 0, by_core)
+    bbulk(lb, lb_sem, 1 - core).wait_recv()
+    pending = hop_sum(hop_done(*pending), 1, by_site)
     ml_ref[...] = jnp.full((1, 1), jnp.sum(lb[...]) / token_count, f32)
 
     def find(j, carry):
@@ -412,18 +445,20 @@
             jnp.where(here == 2 * me, j, a), jnp.where(here == 2 * me + 1, j, b)
         )
 
+    pending = hop_sum(hop_done(*pending), 2, by_z)
     places = lax.fori_loop(0, 2 * n, find, (jnp.int32(0), jnp.int32(0)))
     for off in range(2):
-        slab = lb[lax.div(places[off], 2)]
+        slab = lb[device_slot(lax.div(places[off], 2))]
         odd = lax.rem(places[off], 2)
         tl_ref[off:off + 1, :] = jnp.where(odd == 0, slab[0:1], slab[1:2])
 
-    spread_recv(sqb, sqs, sqr)
-    sq_ref[...] = jnp.sum(sqb[...], axis=0)[0:1, 0:1]
-
-    spread_sent(st, sts, str_)
-    spread_sent(lb, lbs, lbr)
-    spread_sent(sqb, sqs, sqr)
+    sq_ref[...] = hop_done(*pending)[0:1, 0:1]
+
+    bulk_sent(st, st_sem)
+    bulk_sent(lb, lb_sem)
+    for src, hops in enumerate((by_core, by_site, by_z)):
+        for dst, dev in hops:
+            hop(src, dst, dev).wait_send()
     for g in range(PARTS):
         for e in range(1, nz):
             zcopy(g, e, z).wait_send()
@@ -480,7 +515,8 @@
             pltpu.VMEM((2, half_rows, tok), bf16),
             pltpu.VMEM((n, 8, half_tok), f32),
             pltpu.VMEM((n, 8, half_tok), f32),
-            pltpu.VMEM((n, 8, 128), f32),
+            pltpu.VMEM((3, 8, 128), f32),
+            pltpu.VMEM((SITES + nz, 8, 128), f32),
             pltpu.VMEM((CHUNKS, half_rows, cc), bf16),
             pltpu.VMEM((CHUNKS, half_rows, cc), bf16),
             pltpu.VMEM((CHUNKS, SITES, half_rows // SITES, cc), f32),
@@ -492,7 +528,7 @@
             dma((PARTS, nz)), dma((PARTS, nz)),
             dma((PARTS, nz, SITES)), dma((PARTS, nz, SITES)),
             dma((PARTS, nz, SITES)), dma((PARTS, nz, SITES)),
-            dma((n,)), dma((n,)), dma((n,)), dma((n,)), dma((n,)), dma((n,)),
+            dma((2, nz + SITES)), dma((2, nz + SITES)), dma((2, nz + SITES)),
             dma((CHUNKS,)), dma((CHUNKS,)),
             dma((CHUNKS, SITES)), dma((CHUNKS, SITES)),
             dma((CHUNKS, nz)), dma((CHUNKS, nz)),

time: 67.7 us -> 65.9 us (0.973)
  Pallas kernels: 56.6 us -> 54.9 us
    pallas_call x1, Pallas kernels: 56.6 us -> 54.9 us  [fused_body(): pl.pallas_call(functools.partial(kernel, n, shard_rows), out_shape=(jax.S...]
where the time goes in v3:
time: 65.9 us; the launch traced here: 65.7 us
  Pallas kernels  54.9 us (83%)
  matrix products  3.26 us (5%)
  between operations  3.15 us (5%)
  other arithmetic  2.32 us (4%)
  local copies, waits for them, and re-layouts  2.13 us (3%)
    pallas_call x1, Pallas kernels, fused_body(): pl.pallas_call(functools.partial(kernel, n, shard_rows), out_shape=(jax.S...  54.9 us
    dot_general x1, matrix products, fused_body(): jnp.dot(dlogits, rows, preferred_element_type=f32).astype(bf16)  3.26 us
    unnamed x9, local copies, waits for them, and re-layouts  2.13 us

profile of v3, /device:TPU:0, one launch (start us, length us, event | category | flops | bytes accessed | tf_op | source)
XLA Modules:
  0.0 65.7 jit_solution(16326464928869472888)
XLA Ops:
  0.6 0.7 %convert_bitcast_fusion = (f32[2,128]{1,0:T(2,128)S(1)}, f32[2,128]{1,0:T(2,128)S(1)}) fusion(s32[256]{0:T(256)} %param.14, s32[256]{0:T(256)} %param.13), kind=kLoop, calls=%fused_computation.6 | loop fusion | flops 512 | bytes 4096 | tf_op jit(solution)/shard_map/reshape | solution.py:490
  1.3 0.7 %pad_maximum_fusion.stats_ref = f32[8,128]{1,0:T(8,128)S(1)} fusion(f32[2,128]{1,0:T(2,128)} %bitcast.12, f32[2,128]{1,0:T(2,128)} %bitcast.13, f32[2,128]{1,0:T(2,128)S(1)} %get-tuple-element.21, f32[2,128]{1,0:T(2,128)S(1)} %get-tuple-element.22), kind=kLoop, calls=%fused_computation.5 | loop fusion | flops 3072 | bytes 8192 | tf_op jit(solution)/shard_map/concatenate | solution.py:489
  2.0 0.0 copy-start
  2.0 0.9 %copy-done = f32[4,8192]{1,0:T(4,128)S(1)} copy-done((f32[4,8192]{1,0:T(4,128)S(1)}, f32[4,8192]{1,0:T(4,128)}, u32[]{:S(2)}) %copy-start) | copy-done | bytes 131096
  2.9 0.0 copy-start.1
  3.0 0.7 copy-done.1
  3.6 54.9 %shard_map.136 = (f32[2,128]{1,0:T(2,128)S(1)}, f32[1,1]{1,0:T(1,128)}, bf16[128,8192]{1,0:T(8,128)(2,1)S(1)}, bf16[256,128]{1,0:T(8,128)(2,1)S(1)}, f32[4,8192]{1,0:T(4,128)S(1)}, /*index=5*/f32[1,1]{1,0:T(1,128)}) custom-call(s32[64]{0:T(128)S(1)} %copy-done.1, f32[8,128]{1,0:T(8,128)S(1)} %pad_maximum_fusion.stats_ref, f32[4,8192]{1,0:T(4,128)S(1)} %copy-done, ...), custom_call_target="tpu_custom_call" | custom-call | tf_op jit(solution)/shard_map/pallas_call | solution.py:496
  58.5 0.0 copy-start.2
  58.5 0.0 copy-start.3
  58.5 3.3 %convolution_convert_fusion = bf16[256,8192]{1,0:T(8,128)(2,1)} fusion(bf16[256,128]{1,0:T(8,128)(2,1)S(1)} %get-tuple-element.14, bf16[128,8192]{1,0:T(8,128)(2,1)S(1)} %get-tuple-element.15), kind=kOutput, calls=%fused_computation | convolution fusion | flops 538968064 | bytes 6356992 | tf_op jit(solution)/shard_map/dot_general | solution.py:541
  62.4 0.0 copy-done.2
  62.4 0.0 copy-done.3
  62.4 0.9 %multiply_subtract_fusion = (f32[4,8192]{1,0:T(4,128)}, f32[4,8192]{1,0:T(4,128)}, f32[4,8192]{1,0:T(4,128)}) fusion(f32[4,8192]{1,0:T(4,128)S(1)} %copy-done, f32[4,8192]{1,0:T(4,128)S(1)} %get-tuple-element.16, f32[]{:T(128)} %bitcast.6, f32[4,8192]{1,0:T(4,128)S(1)} %copy-done.2, f32[4,8192]{1,0:T(4,128)S(1)} %copy-done.3), kind=kLoop, calls=%fused_computation.3 | loop fusion | flops 458752 | bytes 917508 | tf_op jit(solution)/shard_map/sub | solution.py:547
  63.3 0.6 copy.17
Async XLA Ops:
  2.0 0.9 %copy-start = (f32[4,8192]{1,0:T(4,128)S(1)}, f32[4,8192]{1,0:T(4,128)}, u32[]{:S(2)}) copy-start(f32[4,8192]{1,0:T(4,128)} %mst_hbm.1) | copy-start | bytes 393220
  2.9 0.7 copy-start.1
  58.5 3.9 %copy-start.2 = (f32[4,8192]{1,0:T(4,128)S(1)}, f32[4,8192]{1,0:T(4,128)}, u32[]{:S(2)}) copy-start(f32[4,8192]{1,0:T(4,128)} %param.12) | copy-start | bytes 393220
  58.5 3.9 %copy-start.3 = (f32[4,8192]{1,0:T(4,128)S(1)}, f32[4,8192]{1,0:T(4,128)}, u32[]{:S(2)}) copy-start(f32[4,8192]{1,0:T(4,128)} %param.11) | copy-start | bytes 393220
